TPU v7x, 32 devices: a whole 2x2x4 slice. The times are simulated.
32 devices in a mesh: bead: 2 (over y), row: 4 (over x, core), col: 4 (over z).
Axes of the slice: x: 2, y: 2, z: 4, core: 2. Of those that a mesh axis runs over, the one named last changes fastest.
Arguments:
- tensor_tiles: bfloat16 [256, 3, 128, 3, 128], P(('bead', 'row', 'col')), parts along dimension 0, may hold values from -0.02734375 to 0.02734375
- pair_blocks: int32 [256, 2], P(('bead', 'row', 'col')), parts along dimension 0, may hold values from 0 to 31, as said below
- polarizability: float32 [4096], P('row'), may hold values from 0.3 to 1.2
- direct_field: float32 [3, 8192], P(None, ('bead', 'row')), parts along dimension 1, may hold values from -6 to 6
- cotangent: float32 [3, 8192], P(None, ('bead', 'row')), parts along dimension 1, may hold values from -6 to 6
Outputs:
- dipoles: float32 [3, 8192], P(None, ('bead', 'row')), parts along dimension 1
- field_grad: float32 [3, 8192], P(None, ('bead', 'row')), parts along dimension 1
- tile_grad: bfloat16 [256, 3, 128, 3, 128], P(('bead', 'row', 'col')), parts along dimension 0
There are 2 independent parts, one for each index of `bead`. A program takes and returns all parts, laid end to end along the dimension named above; an argument that names none is the same for every part. Nothing has to cross between parts.
Inputs may be any that keep to these rules, and one draw needn't show every extreme that they name: `pair_blocks`: for pair p, with d = p // 8, the first block lies in [(d // 4) * 8, (d // 4 + 1) * 8) and below 31; the second block is larger than the first.
All inputs are finite; a program needn't handle non-finite values.
Results may differ from a plain program's by a relative error of at most 0.0057.
Values may be sent and summed in bfloat16 or wider, within the bound.
A program may use at most 64 MiB of HBM per device.

v0:
```python
import jax
import jax.numpy as jnp
from jax import lax
from jax.sharding import PartitionSpec as P

ITERS = 3


def per_device(tensor_tiles, pair_blocks, polarizability, direct_field, cotangent):
    row_count = lax.axis_size("row")
    block = tensor_tiles.shape[2]
    local_atoms = polarizability.shape[0]
    local_blocks = local_atoms // block
    total_blocks = local_blocks * row_count
    start = lax.axis_index("row") * local_blocks
    first_block = pair_blocks[:, 0]
    second_block = pair_blocks[:, 1]
    local_first = first_block - start
    row_onehot = (local_first[:, None] == jnp.arange(local_blocks)[None, :]).astype(jnp.float32)

    def dense_columns(col_part):
        col_onehot = (second_block[:, None] == jnp.arange(total_blocks)[None, :]).astype(
            jnp.float32
        )
        col_sum = jnp.einsum("bpj,pn->bnj", col_part, col_onehot, precision=lax.Precision.HIGHEST)
        return col_sum.reshape(3, total_blocks * block)

    def operate(values):
        gathered = lax.all_gather(values, "row", axis=1, tiled=True).reshape(3, total_blocks, block)
        near_side = values.reshape(3, local_blocks, block)[:, local_first]
        far_side = gathered[:, second_block]
        row_part = jnp.einsum(
            "paibj,bpj->api", tensor_tiles, far_side, preferred_element_type=jnp.float32
        )
        col_part = jnp.einsum(
            "paibj,api->bpj", tensor_tiles, near_side, preferred_element_type=jnp.float32
        )
        row_sum = jnp.einsum("api,pr->ari", row_part, row_onehot, precision=lax.Precision.HIGHEST)
        row_sum = row_sum.reshape(3, local_atoms)
        col_sum = dense_columns(col_part)
        mine = lax.psum_scatter(col_sum, "row", scatter_dimension=1, tiled=True) + row_sum
        field = lax.psum(mine, "col")
        return (field, near_side, far_side)

    mu_now = polarizability * direct_field
    mu_near = []
    mu_far = []
    for index in range(ITERS):
        rounded = mu_now.astype(jnp.bfloat16)
        field, near_side, far_side = operate(rounded)
        mu_near.append(near_side)
        mu_far.append(far_side)
        mu_now = polarizability * (direct_field + field)
    adjoint = cotangent
    field_grad = jnp.zeros_like(direct_field)
    w_near = [None] * ITERS
    w_far = [None] * ITERS
    for index in reversed(range(ITERS)):
        weighted = polarizability * adjoint
        field_grad = field_grad + weighted
        adjoint, near_side, far_side = operate(weighted.astype(jnp.bfloat16))
        w_near[index] = near_side
        w_far[index] = far_side
    field_grad = field_grad + polarizability * adjoint
    lefts = jnp.stack(w_near + mu_near)
    rights = jnp.stack(mu_far + w_far)
    tile_grad = jnp.einsum("kapi,kbpj->paibj", lefts, rights, preferred_element_type=jnp.float32)
    return (mu_now, field_grad, tile_grad.astype(jnp.bfloat16))


def solution(mesh):
    placed = (
        P(("bead", "row", "col"), None, None, None, None),
        P(("bead", "row", "col"), None),
        P("row"),
        P(None, ("bead", "row")),
        P(None, ("bead", "row")),
    )
    return jax.shard_map(
        per_device,
        mesh=mesh,
        in_specs=placed,
        out_specs=(
            P(None, ("bead", "row")),
            P(None, ("bead", "row")),
            P(("bead", "row", "col"), None, None, None, None),
        ),
        check_vma=False,
    )
```

profile of v0, /device:TPU:0, one launch (start us, length us, event | category | flops | bytes accessed | tf_op | source)
XLA Modules:
  0.0 291.8 jit_solution(13446382851540095538)
XLA Ops:
  7.2 0.9 fusion.84
  8.1 0.8 multiply_convert_fusion.5
  8.9 0.6 gather_fusion.6
  9.4 0.5 fusion.4
  9.9 0.3 convolution_bitcast_fusion.2
  10.2 2.0 copy.122
  12.2 0.6 gather_fusion
  12.8 0.5 fusion.10
  13.3 0.3 convolution_bitcast_fusion.5
  13.6 2.0 copy.119
  15.6 6.2 %all_gather.21 = bf16[3,4096]{1,0:T(4,128)(2,1)S(1)} all-gather(bf16[3,1024]{1,0:T(4,128)(2,1)S(1)} %get-tuple-element.15), channel_id=1, replica_groups=mesh['bead'=2,'row'=4,'col'=4] {'row'}, dimensions={1}, use_global_device_ids=true | all-gather | bytes 30720 | tf_op jit(solution)/shard_map/all_gather | solution.py:29
  21.8 5.4 %all_gather.18 = bf16[3,4096]{1,0:T(4,128)(2,1)S(1)} all-gather(bf16[3,1024]{1,0:T(4,128)(2,1)S(1)} %get-tuple-element.16), channel_id=1, replica_groups=mesh['bead'=2,'row'=4,'col'=4] {'row'}, dimensions={1}, use_global_device_ids=true | all-gather | bytes 30720 | tf_op jit(solution)/shard_map/all_gather | solution.py:29
  27.2 0.6 gather_fusion.7
  27.8 0.8 fusion.37
  28.5 0.6 gather_fusion.1
  29.1 0.8 fusion.52
  30.0 0.1 convolution_bitcast_fusion.8
  30.3 16.2 %reduce-scatter.25.cloned.1.call-done = f32[1024,3]{1,0:T(8,128)} async-done(((f32[4096,3]{1,0:T(8,128)}), f32[1024,3]{1,0:T(8,128)}) %reduce-scatter.25.cloned.1.call-update) | async-done | bytes 12304
  46.5 1.2 copy.114
  47.7 32.9 %reduce-scatter.19.cloned.1.call-done = f32[1024,3]{1,0:T(8,128)} async-done(((f32[4096,3]{1,0:T(8,128)}), f32[1024,3]{1,0:T(8,128)}) %reduce-scatter.19.cloned.1.call-update) | async-done | bytes 12304
  80.6 1.2 copy.108
  81.9 19.0 %all-reduce.2 = (f32[3,1024]{1,0:T(4,128)S(1)}, f32[3,1024]{1,0:T(4,128)S(1)}) all-reduce(f32[3,1024]{1,0:T(4,128)S(1)} %get-tuple-element.22, f32[3,1024]{1,0:T(4,128)S(1)} %get-tuple-element.21), channel_id=1, replica_groups=mesh['bead'=2,'row'=4,'col'=4] {'col'}, use_global_device_ids=true, to_apply=%region_1.0 | all-reduce | flops 6144 | bytes 49152 | tf_op jit(solution)/shard_map/psum | solution.py:42
  101.0 5.2 %all_gather.19 = bf16[3,4096]{1,0:T(4,128)(2,1)S(1)} all-gather(bf16[3,1024]{1,0:T(4,128)(2,1)S(1)} %get-tuple-element.14), channel_id=1, replica_groups=mesh['bead'=2,'row'=4,'col'=4] {'row'}, dimensions={1}, use_global_device_ids=true | all-gather | bytes 30720 | tf_op jit(solution)/shard_map/all_gather | solution.py:29
  106.1 0.6 gather_fusion.2
  106.7 0.5 fusion.8
  107.2 0.3 convolution_bitcast_fusion.4
  107.5 2.0 copy.120
  109.5 0.6 gather_fusion.3
  110.1 0.8 fusion.47
  110.9 5.2 %all_gather.22 = bf16[3,4096]{1,0:T(4,128)(2,1)S(1)} all-gather(bf16[3,1024]{1,0:T(4,128)(2,1)S(1)} %get-tuple-element.13), channel_id=1, replica_groups=mesh['bead'=2,'row'=4,'col'=4] {'row'}, dimensions={1}, use_global_device_ids=true | all-gather | bytes 30720 | tf_op jit(solution)/shard_map/all_gather | solution.py:29
  116.1 0.6 gather_fusion.8
  116.6 0.5 fusion.2
  117.1 0.3 convolution_bitcast_fusion.1
  117.4 2.0 copy.123
  119.4 0.6 gather_fusion.9
  119.9 0.8 fusion.32
  120.8 0.1 convolution_bitcast_fusion.10
  121.0 0.1 convolution_bitcast_fusion.7
  121.2 17.2 %reduce-scatter.21.cloned.1.call-done = f32[1024,3]{1,0:T(8,128)} async-done(((f32[4096,3]{1,0:T(8,128)}), f32[1024,3]{1,0:T(8,128)}) %reduce-scatter.21.cloned.1.call-update) | async-done | bytes 12304
  138.4 1.2 copy.110
  139.6 32.8 %reduce-scatter.27.cloned.1.call-done = f32[1024,3]{1,0:T(8,128)} async-done(((f32[4096,3]{1,0:T(8,128)}), f32[1024,3]{1,0:T(8,128)}) %reduce-scatter.27.cloned.1.call-update) | async-done | bytes 12304
  172.3 1.2 copy.116
  173.6 19.0 %all-reduce.1 = (f32[3,1024]{1,0:T(4,128)S(1)}, f32[3,1024]{1,0:T(4,128)S(1)}) all-reduce(f32[3,1024]{1,0:T(4,128)S(1)} %bitcast_add_fusion.4, f32[3,1024]{1,0:T(4,128)S(1)} %bitcast_add_fusion.1), channel_id=1, replica_groups=mesh['bead'=2,'row'=4,'col'=4] {'col'}, use_global_device_ids=true, to_apply=%region_3.0 | all-reduce | flops 6144 | bytes 49152 | tf_op jit(solution)/shard_map/psum | solution.py:42
  192.7 5.2 %all_gather.20 = bf16[3,4096]{1,0:T(4,128)(2,1)S(1)} all-gather(bf16[3,1024]{1,0:T(4,128)(2,1)S(1)} %get-tuple-element.12), channel_id=1, replica_groups=mesh['bead'=2,'row'=4,'col'=4] {'row'}, dimensions={1}, use_global_device_ids=true | all-gather | bytes 30720 | tf_op jit(solution)/shard_map/all_gather | solution.py:29
  197.9 0.6 gather_fusion.4
  198.4 0.5 fusion.6
  198.9 0.3 convolution_bitcast_fusion.3
  199.2 2.0 copy.121
  201.2 0.6 gather_fusion.5
  201.8 0.8 fusion.42
  202.6 5.4 %all_gather.23 = bf16[3,4096]{1,0:T(4,128)(2,1)S(1)} all-gather(bf16[3,1024]{1,0:T(4,128)(2,1)S(1)} %get-tuple-element.11), channel_id=1, replica_groups=mesh['bead'=2,'row'=4,'col'=4] {'row'}, dimensions={1}, use_global_device_ids=true | all-gather | bytes 30720 | tf_op jit(solution)/shard_map/all_gather | solution.py:29
  208.0 0.6 gather_fusion.10
  208.5 0.5 fusion
  209.0 0.3 convolution_bitcast_fusion
  209.3 2.0 copy.124
  211.2 0.6 gather_fusion.11
  211.8 0.8 fusion.27
  213.1 2.3 convolution_convert_fusion
  215.5 14.6 %reduce-scatter.23.cloned.1.call-done = f32[1024,3]{1,0:T(8,128)} async-done(((f32[4096,3]{1,0:T(8,128)}), f32[1024,3]{1,0:T(8,128)}) %reduce-scatter.23.cloned.1.call-update) | async-done | bytes 12304
  230.1 1.2 copy.112
  231.3 32.8 %reduce-scatter.29.cloned.1.call-done = f32[1024,3]{1,0:T(8,128)} async-done(((f32[4096,3]{1,0:T(8,128)}), f32[1024,3]{1,0:T(8,128)}) %reduce-scatter.29.cloned.1.call-update) | async-done | bytes 12304
  264.1 1.2 copy.118
  265.3 19.0 %all-reduce = (f32[3,1024]{1,0:T(4,128)S(1)}, f32[3,1024]{1,0:T(4,128)S(1)}) all-reduce(f32[3,1024]{1,0:T(4,128)S(1)} %bitcast_add_fusion.3, f32[3,1024]{1,0:T(4,128)S(1)} %bitcast_add_fusion), channel_id=1, replica_groups=mesh['bead'=2,'row'=4,'col'=4] {'col'}, use_global_device_ids=true, to_apply=%region_5.0 | all-reduce | flops 6144 | bytes 49152 | tf_op jit(solution)/shard_map/psum | solution.py:42
  284.4 0.6 multiply_add_fusion
  (46 shorter events, 1.3 us)
Async XLA Ops:
  7.2 2.3 copy-start
  7.2 39.3 %reduce-scatter.25.cloned.1.call-start = ((), (), s32[]{:S(2)}) async-start(), calls=%async_computation.9 | async-start | bytes 2621440
  12.2 68.4 %reduce-scatter.19.cloned.1.call-start = ((), (), s32[]{:S(2)}) async-start(), calls=%async_computation.6 | async-start | bytes 2621440
  15.6 122.8 %reduce-scatter.21.cloned.1.call-start = ((), (), s32[]{:S(2)}) async-start(), calls=%async_computation.7 | async-start | bytes 2621440
  28.5 72.4 %copy-start.1 = (f32[3,1024]{1,0:T(4,128)S(1)}, f32[3,1024]{1,0:T(4,128)}, u32[]{:S(2)}) copy-start(f32[3,1024]{1,0:T(4,128)} %param.8) | copy-start | bytes 36868
  28.5 72.4 %copy-start.3 = (f32[1024]{0:T(1024)S(1)}, f32[1024]{0:T(1024)}, u32[]{:S(2)}) copy-start(f32[1024]{0:T(1024)} %param.7) | copy-start | bytes 12292
  109.5 62.9 %reduce-scatter.27.cloned.1.call-start = ((), (), s32[]{:S(2)}) async-start(), calls=%async_computation.10 | async-start | bytes 2621440
  121.0 109.1 %reduce-scatter.23.cloned.1.call-start = ((), (), s32[]{:S(2)}) async-start(), calls=%async_computation.8 | async-start | bytes 2621440
  201.2 62.9 %reduce-scatter.29.cloned.1.call-start = ((), (), s32[]{:S(2)}) async-start(), calls=%async_computation.11 | async-start | bytes 2621440
  212.8 71.5 %copy-start.2 = (f32[3,1024]{1,0:T(4,128)S(1)}, f32[3,1024]{1,0:T(4,128)}, u32[]{:S(2)}) copy-start(f32[3,1024]{1,0:T(4,128)} %param.9) | copy-start | bytes 36868
Sparse Core Ops, SparseCore 0:
  12.3 34.1 reduce-scatter.24
  49.2 31.4 reduce-scatter.18
  109.6 28.7 reduce-scatter.20
  140.9 31.3 reduce-scatter.26
  201.3 28.7 reduce-scatter.22
  232.6 31.4 reduce-scatter.28
where the time goes:
time: 292 us
  waiting for transfers between devices  147 us (50%)
  blocking collectives  89.6 us (31%)
  local copies, waits for them, and re-layouts  26.5 us (9%)
  between operations  14.4 us (5%)
  matrix products  12.1 us (4%)
    unnamed x12, waiting for transfers between devices  147 us
    psum x3, blocking collectives, operate(): field = lax.psum(mine, 'col')  57.1 us
    all_gather x6, blocking collectives, operate(): lax.all_gather(values, 'row', axis=1, tiled=True)  32.5 us
    unnamed x20, local copies, waits for them, and re-layouts  19.2 us
  transfers between devices with their start and end apart: 6, of which 6 were waited for; matrix products, arithmetic and copies ran while one was open for 9% of the time, Pallas kernels for 0%

commit v1 on v0

v1 whole, which is shorter than its diff:
```python
import functools

import jax
import jax.numpy as jnp
from jax import lax
from jax.experimental import pallas as pl
from jax.experimental.pallas import tpu as pltpu
from jax.sharding import PartitionSpec as P

ITERS = 3
MESH = pl.DeviceIdType.MESH
UNROLL_LIMIT = 32


def repeat(count, step):
    if count <= UNROLL_LIMIT:
        for index in range(count):
            step(index)
    else:
        lax.fori_loop(0, count, lambda index, carry: (step(index), carry)[1], 0)


def kernel(
    n_row,
    n_col,
    tiles_hbm,
    pairs,
    pol,
    field_in,
    cot_in,
    dip_out,
    grad_out,
    tg_hbm,
    tiles,
    tg,
    source,
    start_send,
    ag_send,
    ag_recv,
    rs_send,
    rs_recv,
    last_send,
    last_recv,
    fields,
    part,
    tile_sem,
    tg_sem,
    ag_send_sem,
    ag_recv_sem,
    rs_send_sem,
    rs_recv_sem,
    last_send_sem,
    last_recv_sem,
):
    group = n_row * n_col
    pair_count = tiles.shape[0]
    block = tiles.shape[3]
    local_blocks = pol.shape[0]
    owned = local_blocks // n_col
    chunk = rs_send.shape[2]
    row = lax.axis_index("row")
    col = lax.axis_index("col")
    me = row * n_col + col

    def peer_of(offset):
        return lax.rem(me + offset, group)

    def place(device):
        return {"row": device // n_col, "col": lax.rem(device, n_col)}

    for p in range(pair_count):
        pltpu.make_async_copy(tiles_hbm.at[p], tiles.at[p], tile_sem.at[p]).start()

    barrier = pltpu.get_barrier_semaphore()

    def greet(index):
        pl.semaphore_signal(
            barrier, inc=1, device_id=place(peer_of(index + 1)), device_id_type=MESH
        )

    repeat(group - 1, greet)

    even = lax.rem(lax.broadcasted_iota(jnp.int32, (8, block), 0), 2) == 0
    start_send[...] = jnp.zeros_like(start_send)
    part[...] = jnp.zeros_like(part)
    for b in range(local_blocks):
        lanes = pl.ds(b * block, block)
        source[b, 6:8, :] = jnp.zeros((2, block), jnp.float32)
        for c in range(3):
            source[b, 2 * c : 2 * c + 1, :] = field_in[c : c + 1, lanes]
            source[b, 2 * c + 1 : 2 * c + 2, :] = cot_in[c : c + 1, lanes]
    for o in range(n_col):
        rows = [pol[b : b + 1, :] * source[b] for b in range(o * owned, (o + 1) * owned)]
        rows += [jnp.zeros((8, block), jnp.float32)] * (chunk // 8 - owned)
        start_send[o] = jnp.concatenate(rows, axis=0).astype(jnp.bfloat16)

    pl.semaphore_wait(barrier, group - 1)

    def start_copy(index):
        other = lax.rem(row + index + 1, n_row)
        return pltpu.make_async_remote_copy(
            src_ref=start_send,
            dst_ref=ag_recv.at[0, pl.ds(row * n_col, n_col)],
            send_sem=ag_send_sem.at[0],
            recv_sem=ag_recv_sem.at[0],
            device_id={"row": other},
            device_id_type=MESH,
        )

    repeat(n_row - 1, lambda index: start_copy(index).start())
    ag_recv[0, pl.ds(row * n_col, n_col)] = start_send[...]

    def wait_for(ref, semaphore):
        pltpu.make_async_copy(ref, ref, semaphore).wait()

    mine = [source[col * owned + i] for i in range(owned)]
    pols = [pol[pl.ds(col * owned + i, 1), :] for i in range(owned)]
    now = [pols[i] * mine[i] for i in range(owned)]
    total = list(now)
    constant = [jnp.where(even, mine[i], 0.0) for i in range(owned)]
    first = [pairs[0, p] for p in range(pair_count)]
    second = [pairs[1, p] for p in range(pair_count)]

    def vector(step, at):
        return jnp.concatenate(
            [fields[step, at, 2 * c : 2 * c + 2, :] for c in range(3)], axis=1
        )

    for step in range(ITERS):
        if step == 0:
            wait_for(ag_recv.at[0, pl.ds(0, (n_row - 1) * n_col)], ag_recv_sem.at[0])
        else:
            wait_for(ag_recv.at[step, pl.ds(0, group - 1)], ag_recv_sem.at[step])

        def unpack(index):
            got = ag_recv[step, index].astype(jnp.float32)
            for i in range(owned):
                fields[step, index * owned + i] = got[8 * i : 8 * i + 8]

        repeat(group, unpack)

        for p in range(pair_count):
            if step == 0:
                pltpu.make_async_copy(tiles_hbm.at[p], tiles.at[p], tile_sem.at[p]).wait()
            near = vector(step, first[p]).astype(jnp.bfloat16)
            far = vector(step, second[p]).astype(jnp.bfloat16)
            tile = jnp.concatenate(
                [
                    jnp.concatenate([tiles[p, a, b] for b in range(3)], axis=1)
                    for a in range(3)
                ],
                axis=0,
            )
            to_second = lax.dot_general(
                near, tile, (((1,), (0,)), ((), ())), preferred_element_type=jnp.float32
            )
            to_first = lax.dot_general(
                far, tile, (((1,), (1,)), ((), ())), preferred_element_type=jnp.float32
            )
            for c in range(3):
                lanes = slice(c * block, (c + 1) * block)
                part[p, 2 * c : 2 * c + 2, :] = to_first[:, lanes]
                part[pair_count + p, 2 * c : 2 * c + 2, :] = to_second[:, lanes]

        terms = [part[i] for i in range(2 * pair_count)]
        ids = [jnp.full((8, block), at, jnp.int32) for at in first + second]

        def gathered(owner):
            sums = []
            for i in range(owned):
                at = owner * owned + i
                got = jnp.zeros((8, block), jnp.float32)
                for term, which in zip(terms, ids):
                    got = got + jnp.where(which == at, term, 0.0)
                sums.append(got)
            return sums

        def send_part(index):
            peer = peer_of(index + 1)
            rows = gathered(peer)
            rows += [jnp.zeros((8, block), jnp.float32)] * (chunk // 8 - owned)
            rs_send[step, peer] = jnp.concatenate(rows, axis=0).astype(jnp.bfloat16)
            pltpu.make_async_remote_copy(
                src_ref=rs_send.at[step, peer],
                dst_ref=rs_recv.at[step, me],
                send_sem=rs_send_sem.at[step],
                recv_sem=rs_recv_sem.at[step],
                device_id=place(peer),
                device_id_type=MESH,
            ).start()

        repeat(group - 1, send_part)
        own = gathered(me)
        rs_recv[step, me] = jnp.zeros((chunk, block), jnp.bfloat16)

        if step == ITERS - 1:
            for p in range(pair_count):
                left, right = [], []
                for t in range(ITERS):
                    left.append(vector(t, first[p]))
                    other = vector(ITERS - 1 - t, second[p])
                    right += [other[1:2], other[0:1]]
                blank = jnp.zeros((2, 3 * block), jnp.float32)
                left = jnp.concatenate(left + [blank], axis=0)
                right = jnp.concatenate(right + [blank], axis=0).astype(jnp.bfloat16)
                for a in range(3):
                    piece = left[:, a * block : (a + 1) * block].T.astype(jnp.bfloat16)
                    outer = jnp.dot(piece, right, preferred_element_type=jnp.float32)
                    for b in range(3):
                        tg[p, a, b] = outer[:, b * block : (b + 1) * block].astype(jnp.bfloat16)
                pltpu.make_async_copy(tg.at[p], tg_hbm.at[p], tg_sem.at[p]).start()

        wait_for(rs_recv.at[step, pl.ds(0, group - 1)], rs_recv_sem.at[step])

        def add(index, sums):
            got = rs_recv[step, index].astype(jnp.float32)
            return tuple(sums[i] + got[8 * i : 8 * i + 8] for i in range(owned))

        if group <= UNROLL_LIMIT:
            sums = tuple(own)
            for index in range(group):
                sums = add(index, sums)
        else:
            sums = lax.fori_loop(0, group, add, tuple(own))
        now = [pols[i] * (constant[i] + sums[i]) for i in range(owned)]
        total = [total[i] + now[i] for i in range(owned)]

        if step < ITERS - 1:
            rows = list(now) + [jnp.zeros((8, block), jnp.float32)] * (chunk // 8 - owned)
            packed = jnp.concatenate(rows, axis=0).astype(jnp.bfloat16)
            ag_send[step] = packed

            def send_field(index):
                pltpu.make_async_remote_copy(
                    src_ref=ag_send.at[step],
                    dst_ref=ag_recv.at[step + 1, me],
                    send_sem=ag_send_sem.at[step + 1],
                    recv_sem=ag_recv_sem.at[step + 1],
                    device_id=place(peer_of(index + 1)),
                    device_id_type=MESH,
                ).start()

            repeat(group - 1, send_field)
            ag_recv[step + 1, me] = packed

    for i in range(owned):
        last_send[i] = jnp.where(even, now[i], total[i])

    def last_copy(index):
        return pltpu.make_async_remote_copy(
            src_ref=last_send,
            dst_ref=last_recv.at[col],
            send_sem=last_send_sem,
            recv_sem=last_recv_sem,
            device_id={"col": lax.rem(col + index + 1, n_col)},
            device_id_type=MESH,
        )

    repeat(n_col - 1, lambda index: last_copy(index).start())
    last_recv[col] = last_send[...]
    wait_for(last_recv.at[pl.ds(0, n_col - 1)], last_recv_sem)
    for b in range(local_blocks):
        lanes = pl.ds(b * block, block)
        for c in range(3):
            dip_out[c : c + 1, lanes] = last_recv[b // owned, b % owned, 2 * c : 2 * c + 1, :]
            grad_out[c : c + 1, lanes] = last_recv[b // owned, b % owned, 2 * c + 1 : 2 * c + 2, :]

    wait_for(ag_recv.at[0, pl.ds(0, (n_row - 1) * n_col)], ag_send_sem.at[0])
    for step in range(ITERS):
        wait_for(rs_send.at[step, pl.ds(0, group - 1)], rs_send_sem.at[step])
        if step > 0:
            wait_for(ag_recv.at[step, pl.ds(0, group - 1)], ag_send_sem.at[step])
    wait_for(last_recv.at[pl.ds(0, n_col - 1)], last_send_sem)
    for p in range(pair_count):
        pltpu.make_async_copy(tg.at[p], tg_hbm.at[p], tg_sem.at[p]).wait()


def per_device(tensor_tiles, pair_blocks, polarizability, direct_field, cotangent):
    n_row = lax.axis_size("row")
    n_col = lax.axis_size("col")
    group = n_row * n_col
    pair_count = tensor_tiles.shape[0]
    block = tensor_tiles.shape[2]
    local_blocks = polarizability.shape[0] // block
    owned = local_blocks // n_col
    chunk = max(16, 8 * owned)
    f32, bf16 = jnp.float32, jnp.bfloat16
    tiles = tensor_tiles.transpose(0, 1, 3, 2, 4)
    vmem = pl.BlockSpec(memory_space=pltpu.VMEM)
    anywhere = pl.BlockSpec(memory_space=pl.ANY)
    dma = pltpu.SemaphoreType.DMA
    dipoles, grad, tile_grad = pl.pallas_call(
        functools.partial(kernel, n_row, n_col),
        out_shape=(
            jax.ShapeDtypeStruct(direct_field.shape, f32),
            jax.ShapeDtypeStruct(direct_field.shape, f32),
            jax.ShapeDtypeStruct(tiles.shape, bf16),
        ),
        in_specs=[anywhere, pl.BlockSpec(memory_space=pltpu.SMEM), vmem, vmem, vmem],
        out_specs=(vmem, vmem, anywhere),
        scratch_shapes=[
            pltpu.VMEM(tiles.shape, bf16),
            pltpu.VMEM(tiles.shape, bf16),
            pltpu.VMEM((local_blocks, 8, block), f32),
            pltpu.VMEM((n_col, chunk, block), bf16),
            pltpu.VMEM((ITERS - 1, chunk, block), bf16),
            pltpu.VMEM((ITERS, group, chunk, block), bf16),
            pltpu.VMEM((ITERS, group, chunk, block), bf16),
            pltpu.VMEM((ITERS, group, chunk, block), bf16),
            pltpu.VMEM((owned, 8, block), f32),
            pltpu.VMEM((n_col, owned, 8, block), f32),
            pltpu.VMEM((ITERS, group * owned, 8, block), f32),
            pltpu.VMEM((2 * pair_count, 8, block), f32),
            dma((pair_count,)),
            dma((pair_count,)),
            dma((ITERS,)),
            dma((ITERS,)),
            dma((ITERS,)),
            dma((ITERS,)),
            dma,
            dma,
        ],
        compiler_params=pltpu.CompilerParams(
            collective_id=0, has_side_effects=True, vmem_limit_bytes=32 * 1024 * 1024
        ),
    )(
        tiles,
        pair_blocks.T,
        polarizability.reshape(local_blocks, block),
        direct_field,
        cotangent,
    )
    return dipoles, grad, tile_grad.transpose(0, 1, 3, 2, 4)


def solution(mesh):
    placed = (
        P(("bead", "row", "col"), None, None, None, None),
        P(("bead", "row", "col"), None),
        P("row"),
        P(None, ("bead", "row")),
        P(None, ("bead", "row")),
    )
    return jax.shard_map(
        per_device,
        mesh=mesh,
        in_specs=placed,
        out_specs=(
            P(None, ("bead", "row")),
            P(None, ("bead", "row")),
            P(("bead", "row", "col"), None, None, None, None),
        ),
        check_vma=False,
    )
```

time: 292 us -> 47.4 us (0.16)
  waiting for transfers between devices: 147 us -> 0 us
  blocking collectives: 89.6 us -> 0 us
  Pallas kernels: 0 us -> 39.3 us
  local copies, waits for them, and re-layouts: 26.5 us -> 7.07 us
  between operations: 14.4 us -> 0.65 us
  matrix products: 12.1 us -> 0 us
    unnamed x12 -> x0, waiting for transfers between devices: 147 us -> none
    psum x3 -> x0, blocking collectives: 57.1 us -> none  [operate(): field = lax.psum(mine, 'col')]
    pallas_call x0 -> x1, Pallas kernels: none -> 39.3 us  [per_device(): pl.pallas_call(functools.partial(kernel, n_row, n_col), out_shape=(jax.Sh...]
    all_gather x6 -> x0, blocking collectives: 32.5 us -> none  [operate(): lax.all_gather(values, 'row', axis=1, tiled=True)]
    dot_general x25 -> x0, matrix products: 12.1 us -> none  [the longest x6 4.64 us: operate(): jnp.einsum('paibj,bpj->api', tensor_tiles, far_side, preferred_element_ty...]
    unnamed x20 -> x13, local copies, waits for them, and re-layouts: 19.2 us -> 7.07 us
    gather x12 -> x0, local copies, waits for them, and re-layouts: 6.93 us -> none  [the longest x6 3.48 us: operate(): far_side = gathered[:, second_block]]
  transfers between devices with their start and end apart: 6 -> 0, of which waited for: 6 -> 0; matrix products, arithmetic and copies ran while one was open for 9% -> 0% of each run, Pallas kernels for 0% -> 0%
where the time goes in v1:
time: 47.4 us; the launch traced here: 47.1 us
  Pallas kernels  39.3 us (83%)
  local copies, waits for them, and re-layouts  7.07 us (15%)
  between operations  0.65 us (1%)
    pallas_call x1, Pallas kernels, per_device(): pl.pallas_call(functools.partial(kernel, n_row, n_col), out_shape=(jax.Sh...  39.3 us
    unnamed x13, local copies, waits for them, and re-layouts  7.07 us

profile of v1, /device:TPU:0, one launch (start us, length us, event | category | flops | bytes accessed | tf_op | source)
XLA Modules:
  0.0 47.1 jit_solution(13822075222062312808)
XLA Ops:
  0.6 0.0 copy-start
  0.6 1.7 %copy-done = bf16[8,3,128,3,128]{4,2,3,1,0:T(8,128)(2,1)S(1)} copy-done((bf16[8,3,128,3,128]{4,2,3,1,0:T(8,128)(2,1)S(1)}, bf16[8,3,128,3,128]{4,2,3,1,0:T(8,128)(2,1)}, u32[]{:S(2)}) %copy-start) | copy-done | bytes 2359320
  2.3 0.0 copy-start.1
  2.3 0.7 %copy-done.1 = f32[3,1024]{1,0:T(4,128)S(1)} copy-done((f32[3,1024]{1,0:T(4,128)S(1)}, f32[3,1024]{1,0:T(4,128)}, u32[]{:S(2)}) %copy-start.1) | copy-done | bytes 12312
  3.0 0.0 copy-start.2
  3.0 0.7 %copy-done.2 = f32[3,1024]{1,0:T(4,128)S(1)} copy-done((f32[3,1024]{1,0:T(4,128)S(1)}, f32[3,1024]{1,0:T(4,128)}, u32[]{:S(2)}) %copy-start.2) | copy-done | bytes 12312
  3.7 0.0 copy-start.3
  3.7 0.7 %copy-done.3 = f32[1024]{0:T(1024)S(1)} copy-done((f32[1024]{0:T(1024)S(1)}, f32[1024]{0:T(1024)}, u32[]{:S(2)}) %copy-start.3) | copy-done | bytes 4120
  4.4 0.0 copy-start.4
  4.4 0.7 %copy-done.4 = s32[8,2]{0,1:T(2,128)S(1)} copy-done((s32[8,2]{0,1:T(2,128)S(1)}, s32[8,2]{0,1:T(2,128)}, u32[]{:S(2)}) %copy-start.4) | copy-done | bytes 88
  5.1 39.3 %shard_map.76 = (f32[3,1024]{1,0:T(4,128)S(1)}, f32[3,1024]{1,0:T(4,128)S(1)}, bf16[8,3,3,128,128]{4,3,2,1,0:T(8,128)(2,1)S(1)}) custom-call(bf16[8,3,3,128,128]{4,3,2,1,0:T(8,128)(2,1)S(1)} %bitcast.4, s32[2,8]{1,0:T(2,128)S(1)} %bitcast.7, f32[8,128]{1,0:T(8,128)S(1)} %bitcast.6, f32[3,1024]{1,0:T(4,128)S(1)} %copy-done.1, f32[3,1024]{1,0:T(4,128)S(1)} %copy-done.2), custom_call_target="tpu_custom_call" | custom-call | tf_op jit(solution)/shard_map/pallas_call | solution.py:292
  44.4 0.6 %copy.11 = f32[3,1024]{1,0:T(4,128)} copy(f32[3,1024]{1,0:T(4,128)S(1)} %get-tuple-element.12) | data formatting | bytes 24576
  45.0 0.6 %copy.12 = f32[3,1024]{1,0:T(4,128)} copy(f32[3,1024]{1,0:T(4,128)S(1)} %get-tuple-element.13) | data formatting | bytes 24576
  45.6 1.4 %copy.13 = bf16[8,3,128,3,128]{4,2,3,1,0:T(8,128)(2,1)} copy(bf16[8,3,128,3,128]{4,2,3,1,0:T(8,128)(2,1)S(1)} %bitcast.5) | data formatting | bytes 4718592
Async XLA Ops:
  0.6 1.7 %copy-start = (bf16[8,3,128,3,128]{4,2,3,1,0:T(8,128)(2,1)S(1)}, bf16[8,3,128,3,128]{4,2,3,1,0:T(8,128)(2,1)}, u32[]{:S(2)}) copy-start(bf16[8,3,128,3,128]{4,2,3,1,0:T(8,128)(2,1)} %param.5) | copy-start | bytes 7077892
  2.3 0.7 %copy-start.1 = (f32[3,1024]{1,0:T(4,128)S(1)}, f32[3,1024]{1,0:T(4,128)}, u32[]{:S(2)}) copy-start(f32[3,1024]{1,0:T(4,128)} %field_in.1) | copy-start | bytes 36868
  3.0 0.7 %copy-start.2 = (f32[3,1024]{1,0:T(4,128)S(1)}, f32[3,1024]{1,0:T(4,128)}, u32[]{:S(2)}) copy-start(f32[3,1024]{1,0:T(4,128)} %cot_in.1) | copy-start | bytes 36868
  3.7 0.7 %copy-start.3 = (f32[1024]{0:T(1024)S(1)}, f32[1024]{0:T(1024)}, u32[]{:S(2)}) copy-start(f32[1024]{0:T(1024)} %param.7) | copy-start | bytes 12292
  4.4 0.7 %copy-start.4 = (s32[8,2]{0,1:T(2,128)S(1)}, s32[8,2]{0,1:T(2,128)}, u32[]{:S(2)}) copy-start(s32[8,2]{0,1:T(2,128)} %param.6) | copy-start | bytes 196

commit v2 on v0

v2 whole, which is shorter than its diff:
```python
import functools

import jax
import jax.numpy as jnp
from jax import lax
from jax.experimental import pallas as pl
from jax.experimental.pallas import tpu as pltpu
from jax.sharding import PartitionSpec as P

ITERS = 3
MESH = pl.DeviceIdType.MESH
UNROLL_LIMIT = 32


def repeat(count, step):
    if count <= UNROLL_LIMIT:
        for index in range(count):
            step(index)
    else:
        lax.fori_loop(0, count, lambda index, carry: (step(index), carry)[1], 0)


def loop(start, end, step):
    lax.fori_loop(start, end, lambda index, carry: (step(index), carry)[1], 0)


def kernel(
    n_row,
    n_col,
    tiles_hbm,
    pairs_hbm,
    pol_hbm,
    field_hbm,
    cot_hbm,
    dip_out,
    grad_out,
    tg_out,
    tiles,
    tg,
    dip,
    grad,
    pairs,
    pol,
    field_in,
    cot_in,
    stage,
    ag_send,
    ag_recv,
    rs_send,
    rs_recv,
    fields,
    part,
    tile_sem,
    tg_sem,
    in_sem,
    out_sem,
    ag_send_sem,
    ag_recv_sem,
    rs_send_sem,
    rs_recv_sem,
):
    group = n_row * n_col
    pair_count = tiles.shape[0]
    block = tiles.shape[3]
    local_blocks = pol.shape[0]
    chunk = ag_send.shape[1]
    row = lax.axis_index("row")
    col = lax.axis_index("col")
    me = row * n_col + col

    inputs = [
        pltpu.make_async_copy(source, target, in_sem.at[index])
        for index, (source, target) in enumerate(
            ((pairs_hbm, pairs), (pol_hbm, pol), (field_hbm, field_in), (cot_hbm, cot_in))
        )
    ]
    tile_copies = [
        pltpu.make_async_copy(tiles_hbm.at[p], tiles.at[p], tile_sem.at[p])
        for p in range(pair_count)
    ]
    barrier = pltpu.get_barrier_semaphore()

    def greet(index):
        peer = lax.rem(me + index + 1, group)
        pl.semaphore_signal(
            barrier,
            inc=1,
            device_id={"row": peer // n_col, "col": lax.rem(peer, n_col)},
            device_id_type=MESH,
        )

    repeat(group - 1, greet)
    for copy in inputs + tile_copies:
        copy.start()
    for copy in inputs:
        copy.wait()

    index = lax.broadcasted_iota(jnp.int32, (chunk, block), 0)
    even = lax.rem(index, 2) == 0
    stage[...] = jnp.zeros_like(stage)
    part[...] = jnp.zeros_like(part)
    for b in range(local_blocks):
        lanes = pl.ds(b * block, block)
        for c in range(3):
            at = 6 * b + 2 * c
            stage[0, at : at + 1, :] = field_in[c : c + 1, lanes]
            stage[0, at + 1 : at + 2, :] = cot_in[c : c + 1, lanes]
        stage[1, 6 * b : 6 * b + 6, :] = jnp.broadcast_to(pol[b : b + 1, :], (6, block))
    source = stage[0]
    pols = stage[1]
    now = pols * source
    total = now
    constant = jnp.where(even, source, 0.0)
    first = [pairs[0, p] for p in range(pair_count)]
    second = [pairs[1, p] for p in range(pair_count)]
    first_ids = [jnp.full((8, block), at, jnp.int32) for at in first]
    second_ids = [jnp.full((8, block), at, jnp.int32) for at in second]

    def wait_for(ref, semaphore):
        pltpu.make_async_copy(ref, ref, semaphore).wait()

    def vector(step, at):
        return jnp.concatenate(
            [fields[step, at, 2 * c : 2 * c + 2, :] for c in range(3)], axis=1
        )

    def unpack(step, which_row, packed):
        stage[2] = packed.astype(jnp.float32)
        for b in range(local_blocks):
            fields[step, which_row * local_blocks + b, 0:6, :] = stage[2, 6 * b : 6 * b + 6, :]

    def matrix(p):
        return jnp.concatenate(
            [
                jnp.concatenate([tiles[p, a, b] for b in range(3)], axis=1)
                for a in range(3)
            ],
            axis=0,
        )

    def keep(slot, values):
        for c in range(3):
            part[slot, 2 * c : 2 * c + 2, :] = values[:, c * block : (c + 1) * block]

    def summed(which_row, slots, ids):
        terms = [part[slot] for slot in slots]
        for b in range(local_blocks):
            at = which_row * local_blocks + b
            got = jnp.where(ids[0] == at, terms[0], 0.0)
            for term, which in zip(terms[1:], ids[1:]):
                got = got + jnp.where(which == at, term, 0.0)
            stage[3, 6 * b : 6 * b + 6, :] = got[0:6]
        return stage[3].astype(jnp.bfloat16)

    def part_copy(step, target_row, target_col):
        return pltpu.make_async_remote_copy(
            src_ref=rs_send.at[step, target_row],
            dst_ref=rs_recv.at[step, row, col],
            send_sem=rs_send_sem.at[step, target_row],
            recv_sem=rs_recv_sem.at[step, row],
            device_id={"row": target_row, "col": target_col},
            device_id_type=MESH,
        )

    pl.semaphore_wait(barrier, group - 1)

    for step in range(ITERS):
        packed = now.astype(jnp.bfloat16)
        ag_send[step] = packed

        def send_field(index):
            pltpu.make_async_remote_copy(
                src_ref=ag_send.at[step],
                dst_ref=ag_recv.at[step, row],
                send_sem=ag_send_sem.at[step],
                recv_sem=ag_recv_sem.at[step],
                device_id={"row": lax.rem(row + index + 1, n_row)},
                device_id_type=MESH,
            ).start()

        repeat(n_row - 1, send_field)
        ag_recv[step, row] = packed
        unpack(step, row, packed)

        for p in range(pair_count):
            if step == 0:
                tile_copies[p].wait()
            near = vector(step, first[p]).astype(jnp.bfloat16)
            keep(
                pair_count + p,
                lax.dot_general(
                    near,
                    matrix(p),
                    (((1,), (0,)), ((), ())),
                    preferred_element_type=jnp.float32,
                ),
            )

        def send_later(back):
            target = n_row - 1 - back
            rs_send[step, target] = summed(
                target, range(pair_count, 2 * pair_count), second_ids
            )
            for k in range(n_col):
                part_copy(step, target, lax.rem(col + k, n_col)).start()

        loop(0, n_row - 1 - row, send_later)

        wait_for(ag_recv.at[step, pl.ds(0, n_row - 1)], ag_recv_sem.at[step])
        repeat(n_row, lambda index: unpack(step, index, ag_recv[step, index]))
        for p in range(pair_count):
            far = vector(step, second[p]).astype(jnp.bfloat16)
            keep(
                p,
                lax.dot_general(
                    far,
                    matrix(p),
                    (((1,), (1,)), ((), ())),
                    preferred_element_type=jnp.float32,
                ),
            )
        own = summed(row, range(2 * pair_count), first_ids + second_ids)
        rs_send[step, row] = own
        for k in range(1, n_col):
            part_copy(step, row, lax.rem(col + k, n_col)).start()
        rs_recv[step, row, col] = own

        if step == ITERS - 1:
            for p in range(pair_count):
                left, right = [], []
                for t in range(ITERS):
                    left.append(vector(t, first[p]))
                    other = vector(ITERS - 1 - t, second[p])
                    right += [other[1:2], other[0:1]]
                blank = jnp.zeros((2, 3 * block), jnp.float32)
                left = jnp.concatenate(left + [blank], axis=0)
                right = jnp.concatenate(right + [blank], axis=0).astype(jnp.bfloat16)
                for a in range(3):
                    piece = left[:, a * block : (a + 1) * block].T.astype(jnp.bfloat16)
                    outer = jnp.dot(piece, right, preferred_element_type=jnp.float32)
                    for b in range(3):
                        tg[p, a, b] = outer[:, b * block : (b + 1) * block].astype(jnp.bfloat16)
                pltpu.make_async_copy(tg.at[p], tg_out.at[p], tg_sem.at[p]).start()

        def add_row(source_row, sums):
            for c in range(n_col):
                sums = sums + rs_recv[step, source_row, c].astype(jnp.float32)
            return sums

        def take(source_row, sums):
            wait_for(
                rs_recv.at[step, 0, pl.ds(0, n_col)], rs_recv_sem.at[step, source_row]
            )
            return add_row(source_row, sums)

        sums = lax.fori_loop(0, row, take, jnp.zeros((chunk, block), jnp.float32))
        wait_for(rs_recv.at[step, 0, pl.ds(0, n_col - 1)], rs_recv_sem.at[step, row])
        now = pols * (constant + add_row(row, sums))
        total = total + now

    stage[2] = now
    stage[3] = total
    for b in range(local_blocks):
        lanes = pl.ds(b * block, block)
        for c in range(3):
            at = 6 * b + 2 * c
            dip[c : c + 1, lanes] = stage[2, at : at + 1, :]
            grad[c : c + 1, lanes] = stage[3, at + 1 : at + 2, :]
    results = [
        pltpu.make_async_copy(dip, dip_out, out_sem.at[0]),
        pltpu.make_async_copy(grad, grad_out, out_sem.at[1]),
    ]
    for copy in results:
        copy.start()

    for step in range(ITERS):
        wait_for(ag_recv.at[step, pl.ds(0, n_row - 1)], ag_send_sem.at[step])
        wait_for(rs_recv.at[step, 0, pl.ds(0, n_col - 1)], rs_send_sem.at[step, row])
        loop(
            row + 1,
            n_row,
            lambda target: wait_for(
                rs_recv.at[step, 0, pl.ds(0, n_col)], rs_send_sem.at[step, target]
            ),
        )
    for p in range(pair_count):
        pltpu.make_async_copy(tg.at[p], tg_out.at[p], tg_sem.at[p]).wait()
    for copy in results:
        copy.wait()


def copy_out(dip, grad, tg, dip_out, grad_out, tg_out, dip_held, grad_held, tg_held, sems):
    pieces = [(tg.at[p], tg_held.at[p], tg_out.at[p]) for p in range(tg.shape[0])]
    pieces += [(dip, dip_held, dip_out), (grad, grad_held, grad_out)]
    loads = [
        pltpu.make_async_copy(source, held, sems.at[0, i])
        for i, (source, held, _) in enumerate(pieces)
    ]
    stores = [
        pltpu.make_async_copy(held, target, sems.at[1, i])
        for i, (_, held, target) in enumerate(pieces)
    ]
    for load in loads:
        load.start()
    for load, store in zip(loads, stores):
        load.wait()
        store.start()
    for store in stores:
        store.wait()


def per_device(tensor_tiles, pair_blocks, polarizability, direct_field, cotangent):
    n_row = lax.axis_size("row")
    n_col = lax.axis_size("col")
    pair_count = tensor_tiles.shape[0]
    block = tensor_tiles.shape[2]
    local_blocks = polarizability.shape[0] // block
    chunk = -(-6 * local_blocks // 16) * 16
    f32, bf16 = jnp.float32, jnp.bfloat16
    tiles = tensor_tiles.transpose(0, 1, 3, 2, 4)
    hbm = pl.BlockSpec(memory_space=pltpu.HBM)
    anywhere = pl.BlockSpec(memory_space=pl.ANY)
    dma = pltpu.SemaphoreType.DMA
    shapes = (
        jax.ShapeDtypeStruct(direct_field.shape, f32),
        jax.ShapeDtypeStruct(direct_field.shape, f32),
        jax.ShapeDtypeStruct(tiles.shape, bf16),
    )
    results = pl.pallas_call(
        functools.partial(kernel, n_row, n_col),
        out_shape=shapes,
        in_specs=[hbm] * 5,
        out_specs=(anywhere,) * 3,
        scratch_shapes=[
            pltpu.VMEM(tiles.shape, bf16),
            pltpu.VMEM(tiles.shape, bf16),
            pltpu.VMEM(direct_field.shape, f32),
            pltpu.VMEM(direct_field.shape, f32),
            pltpu.SMEM((2, pair_count), jnp.int32),
            pltpu.VMEM((local_blocks, block), f32),
            pltpu.VMEM(direct_field.shape, f32),
            pltpu.VMEM(direct_field.shape, f32),
            pltpu.VMEM((4, chunk, block), f32),
            pltpu.VMEM((ITERS, chunk, block), bf16),
            pltpu.VMEM((ITERS, n_row, chunk, block), bf16),
            pltpu.VMEM((ITERS, n_row, chunk, block), bf16),
            pltpu.VMEM((ITERS, n_row, n_col, chunk, block), bf16),
            pltpu.VMEM((ITERS, n_row * local_blocks, 8, block), f32),
            pltpu.VMEM((2 * pair_count, 8, block), f32),
            dma((pair_count,)),
            dma((pair_count,)),
            dma((4,)),
            dma((2,)),
            dma((ITERS,)),
            dma((ITERS,)),
            dma((ITERS, n_row)),
            dma((ITERS, n_row)),
        ],
        compiler_params=pltpu.CompilerParams(
            collective_id=0, has_side_effects=True, vmem_limit_bytes=60 * 1024 * 1024
        ),
    )(
        tiles,
        pair_blocks.T,
        polarizability.reshape(local_blocks, block),
        direct_field,
        cotangent,
    )
    dipoles, grad, tile_grad = pl.pallas_call(
        copy_out,
        out_shape=shapes,
        in_specs=[anywhere] * 3,
        out_specs=(anywhere,) * 3,
        scratch_shapes=[
            pltpu.VMEM(direct_field.shape, f32),
            pltpu.VMEM(direct_field.shape, f32),
            pltpu.VMEM(tiles.shape, bf16),
            dma((2, pair_count + 2)),
        ],
    )(*results)
    return dipoles, grad, tile_grad.transpose(0, 1, 3, 2, 4)


def solution(mesh):
    placed = (
        P(("bead", "row", "col"), None, None, None, None),
        P(("bead", "row", "col"), None),
        P("row"),
        P(None, ("bead", "row")),
        P(None, ("bead", "row")),
    )
    return jax.shard_map(
        per_device,
        mesh=mesh,
        in_specs=placed,
        out_specs=(
            P(None, ("bead", "row")),
            P(None, ("bead", "row")),
            P(("bead", "row", "col"), None, None, None, None),
        ),
        check_vma=False,
    )
```

time: 292 us -> 31.8 us (0.11)
  waiting for transfers between devices: 147 us -> 0 us
  blocking collectives: 89.6 us -> 0 us
  Pallas kernels: 0 us -> 31 us
  local copies, waits for them, and re-layouts: 26.5 us -> 0 us
  between operations: 14.4 us -> 0.64 us
  matrix products: 12.1 us -> 0 us
    unnamed x12 -> x0, waiting for transfers between devices: 147 us -> none
    psum x3 -> x0, blocking collectives: 57.1 us -> none  [operate(): field = lax.psum(mine, 'col')]
    all_gather x6 -> x0, blocking collectives: 32.5 us -> none  [operate(): lax.all_gather(values, 'row', axis=1, tiled=True)]
    pallas_call x0 -> x2, Pallas kernels: none -> 31 us  [the longest x1 28.5 us: per_device(): pl.pallas_call(functools.partial(kernel, n_row, n_col), out_shape=shapes,...]
    unnamed x20 -> x0, local copies, waits for them, and re-layouts: 19.2 us -> none
    dot_general x25 -> x0, matrix products: 12.1 us -> none  [the longest x6 4.64 us: operate(): jnp.einsum('paibj,bpj->api', tensor_tiles, far_side, preferred_element_ty...]
    gather x12 -> x0, local copies, waits for them, and re-layouts: 6.93 us -> none  [the longest x6 3.48 us: operate(): far_side = gathered[:, second_block]]
  transfers between devices with their start and end apart: 6 -> 0, of which waited for: 6 -> 0; matrix products, arithmetic and copies ran while one was open for 9% -> 0% of each run, Pallas kernels for 0% -> 0%
where the time goes in v2:
time: 31.8 us; the launch traced here: 31.6 us
  Pallas kernels  31 us (97%)
  between operations  0.64 us (2%)
    pallas_call x1, Pallas kernels, per_device(): pl.pallas_call(functools.partial(kernel, n_row, n_col), out_shape=shapes,...  28.5 us
    pallas_call x1, Pallas kernels, per_device(): pl.pallas_call(copy_out, out_shape=shapes, in_specs=[anywhere] * 3, out_s...  2.54 us

profile of v2, /device:TPU:0, one launch (start us, length us, event | category | flops | bytes accessed | tf_op | source)
XLA Modules:
  0.0 31.6 jit_solution(9850328191974595434)
XLA Ops:
  0.6 28.5 %shard_map.76 = (f32[3,1024]{1,0:T(4,128)}, f32[3,1024]{1,0:T(4,128)}, bf16[8,3,3,128,128]{4,3,2,1,0:T(8,128)(2,1)}) custom-call(bf16[8,3,3,128,128]{4,3,2,1,0:T(8,128)(2,1)} %bitcast.4, s32[2,8]{1,0:T(2,128)} %bitcast.6, f32[8,128]{1,0:T(8,128)} %bitcast.5, f32[3,1024]{1,0:T(4,128)} %field_hbm.1, f32[3,1024]{1,0:T(4,128)} %cot_hbm.1), custom_call_target="tpu_custom_call" | custom-call | tf_op jit(solution)/shard_map/pallas_call | solution.py:329
  29.1 2.5 %shard_map.77 = (f32[3,1024]{1,0:T(4,128)}, f32[3,1024]{1,0:T(4,128)}, bf16[8,3,3,128,128]{4,3,2,1,0:T(8,128)(2,1)}) custom-call(f32[3,1024]{1,0:T(4,128)} %get-tuple-element.9.dip, f32[3,1024]{1,0:T(4,128)} %get-tuple-element.10.grad, bf16[8,3,3,128,128]{4,3,2,1,0:T(8,128)(2,1)} %get-tuple-element.11.tg), custom_call_target="tpu_custom_call" | custom-call | tf_op jit(solution)/shard_map/pallas_call | solution.py:369

commit v3 on v2

--- a/solution.py
+++ b/solution.py
@@ -32,13 +32,10 @@
     pol_hbm,
     field_hbm,
     cot_hbm,
-    dip_out,
-    grad_out,
-    tg_out,
-    tiles,
-    tg,
     dip,
     grad,
+    tg,
+    tiles,
     pairs,
     pol,
     field_in,
@@ -51,9 +48,7 @@
     fields,
     part,
     tile_sem,
-    tg_sem,
     in_sem,
-    out_sem,
     ag_send_sem,
     ag_recv_sem,
     rs_send_sem,
@@ -150,7 +145,7 @@
             for term, which in zip(terms[1:], ids[1:]):
                 got = got + jnp.where(which == at, term, 0.0)
             stage[3, 6 * b : 6 * b + 6, :] = got[0:6]
-        return stage[3].astype(jnp.bfloat16)
+        return stage[3]
 
     def part_copy(step, target_row, target_col):
         return pltpu.make_async_remote_copy(
@@ -168,18 +163,17 @@
         packed = now.astype(jnp.bfloat16)
         ag_send[step] = packed
 
-        def send_field(index):
+        def send_field(target):
             pltpu.make_async_remote_copy(
                 src_ref=ag_send.at[step],
                 dst_ref=ag_recv.at[step, row],
-                send_sem=ag_send_sem.at[step],
-                recv_sem=ag_recv_sem.at[step],
-                device_id={"row": lax.rem(row + index + 1, n_row)},
+                send_sem=ag_send_sem.at[step, target],
+                recv_sem=ag_recv_sem.at[step, row],
+                device_id={"row": target},
                 device_id_type=MESH,
             ).start()
 
-        repeat(n_row - 1, send_field)
-        ag_recv[step, row] = packed
+        loop(0, row, send_field)
         unpack(step, row, packed)
 
         for p in range(pair_count):
@@ -198,16 +192,20 @@
 
         def send_later(back):
             target = n_row - 1 - back
-            rs_send[step, target] = summed(
-                target, range(pair_count, 2 * pair_count), second_ids
-            )
+            later = summed(target, range(pair_count, 2 * pair_count), second_ids)
+            rs_send[step, target] = later.astype(jnp.bfloat16)
             for k in range(n_col):
                 part_copy(step, target, lax.rem(col + k, n_col)).start()
 
         loop(0, n_row - 1 - row, send_later)
 
-        wait_for(ag_recv.at[step, pl.ds(0, n_row - 1)], ag_recv_sem.at[step])
-        repeat(n_row, lambda index: unpack(step, index, ag_recv[step, index]))
+        stage[4] = summed(row, range(pair_count, 2 * pair_count), second_ids)
+
+        def take_field(source_row):
+            wait_for(ag_send.at[step], ag_recv_sem.at[step, source_row])
+            unpack(step, source_row, ag_recv[step, source_row])
+
+        loop(row + 1, n_row, take_field)
         for p in range(pair_count):
             far = vector(step, second[p]).astype(jnp.bfloat16)
             keep(
@@ -219,7 +217,7 @@
                     preferred_element_type=jnp.float32,
                 ),
             )
-        own = summed(row, range(2 * pair_count), first_ids + second_ids)
+        own = (stage[4] + summed(row, range(pair_count), first_ids)).astype(jnp.bfloat16)
         rs_send[step, row] = own
         for k in range(1, n_col):
             part_copy(step, row, lax.rem(col + k, n_col)).start()
@@ -240,7 +238,6 @@
                     outer = jnp.dot(piece, right, preferred_element_type=jnp.float32)
                     for b in range(3):
                         tg[p, a, b] = outer[:, b * block : (b + 1) * block].astype(jnp.bfloat16)
-                pltpu.make_async_copy(tg.at[p], tg_out.at[p], tg_sem.at[p]).start()
 
         def add_row(source_row, sums):
             for c in range(n_col):
@@ -266,15 +263,9 @@
             at = 6 * b + 2 * c
             dip[c : c + 1, lanes] = stage[2, at : at + 1, :]
             grad[c : c + 1, lanes] = stage[3, at + 1 : at + 2, :]
-    results = [
-        pltpu.make_async_copy(dip, dip_out, out_sem.at[0]),
-        pltpu.make_async_copy(grad, grad_out, out_sem.at[1]),
-    ]
-    for copy in results:
-        copy.start()
 
     for step in range(ITERS):
-        wait_for(ag_recv.at[step, pl.ds(0, n_row - 1)], ag_send_sem.at[step])
+        loop(0, row, lambda target: wait_for(ag_send.at[step], ag_send_sem.at[step, target]))
         wait_for(rs_recv.at[step, 0, pl.ds(0, n_col - 1)], rs_send_sem.at[step, row])
         loop(
             row + 1,
@@ -283,30 +274,17 @@
                 rs_recv.at[step, 0, pl.ds(0, n_col)], rs_send_sem.at[step, target]
             ),
         )
-    for p in range(pair_count):
-        pltpu.make_async_copy(tg.at[p], tg_out.at[p], tg_sem.at[p]).wait()
-    for copy in results:
+
+
+def copy_out(*refs):
+    count = (len(refs) - 1) // 2
+    copies = [
+        pltpu.make_async_copy(refs[i], refs[count + i], refs[-1].at[i]) for i in range(count)
+    ]
+    for copy in copies[::-1]:
+        copy.start()
+    for copy in copies:
         copy.wait()
-
-
-def copy_out(dip, grad, tg, dip_out, grad_out, tg_out, dip_held, grad_held, tg_held, sems):
-    pieces = [(tg.at[p], tg_held.at[p], tg_out.at[p]) for p in range(tg.shape[0])]
-    pieces += [(dip, dip_held, dip_out), (grad, grad_held, grad_out)]
-    loads = [
-        pltpu.make_async_copy(source, held, sems.at[0, i])
-        for i, (source, held, _) in enumerate(pieces)
-    ]
-    stores = [
-        pltpu.make_async_copy(held, target, sems.at[1, i])
-        for i, (_, held, target) in enumerate(pieces)
-    ]
-    for load in loads:
-        load.start()
-    for load, store in zip(loads, stores):
-        load.wait()
-        store.start()
-    for store in stores:
-        store.wait()
 
 
 def per_device(tensor_tiles, pair_blocks, polarizability, direct_field, cotangent):
@@ -318,6 +296,7 @@
     chunk = -(-6 * local_blocks // 16) * 16
     f32, bf16 = jnp.float32, jnp.bfloat16
     tiles = tensor_tiles.transpose(0, 1, 3, 2, 4)
+    vmem = pl.BlockSpec(memory_space=pltpu.VMEM)
     hbm = pl.BlockSpec(memory_space=pltpu.HBM)
     anywhere = pl.BlockSpec(memory_space=pl.ANY)
     dma = pltpu.SemaphoreType.DMA
@@ -328,19 +307,16 @@
     )
     results = pl.pallas_call(
         functools.partial(kernel, n_row, n_col),
-        out_shape=shapes,
+        out_shape=tuple(pltpu.VMEM(x.shape, x.dtype) for x in shapes),
         in_specs=[hbm] * 5,
-        out_specs=(anywhere,) * 3,
+        out_specs=(vmem,) * 3,
         scratch_shapes=[
             pltpu.VMEM(tiles.shape, bf16),
-            pltpu.VMEM(tiles.shape, bf16),
-            pltpu.VMEM(direct_field.shape, f32),
-            pltpu.VMEM(direct_field.shape, f32),
             pltpu.SMEM((2, pair_count), jnp.int32),
             pltpu.VMEM((local_blocks, block), f32),
             pltpu.VMEM(direct_field.shape, f32),
             pltpu.VMEM(direct_field.shape, f32),
-            pltpu.VMEM((4, chunk, block), f32),
+            pltpu.VMEM((5, chunk, block), f32),
             pltpu.VMEM((ITERS, chunk, block), bf16),
             pltpu.VMEM((ITERS, n_row, chunk, block), bf16),
             pltpu.VMEM((ITERS, n_row, chunk, block), bf16),
@@ -348,11 +324,9 @@
             pltpu.VMEM((ITERS, n_row * local_blocks, 8, block), f32),
             pltpu.VMEM((2 * pair_count, 8, block), f32),
             dma((pair_count,)),
-            dma((pair_count,)),
             dma((4,)),
-            dma((2,)),
-            dma((ITERS,)),
-            dma((ITERS,)),
+            dma((ITERS, n_row)),
+            dma((ITERS, n_row)),
             dma((ITERS, n_row)),
             dma((ITERS, n_row)),
         ],
@@ -369,14 +343,10 @@
     dipoles, grad, tile_grad = pl.pallas_call(
         copy_out,
         out_shape=shapes,
-        in_specs=[anywhere] * 3,
+        in_specs=[vmem] * 3,
         out_specs=(anywhere,) * 3,
-        scratch_shapes=[
-            pltpu.VMEM(direct_field.shape, f32),
-            pltpu.VMEM(direct_field.shape, f32),
-            pltpu.VMEM(tiles.shape, bf16),
-            dma((2, pair_count + 2)),
-        ],
+        scratch_shapes=[dma((3,))],
+        compiler_params=pltpu.CompilerParams(vmem_limit_bytes=32 * 1024 * 1024),
     )(*results)
     return dipoles, grad, tile_grad.transpose(0, 1, 3, 2, 4)
 

time: 31.8 us -> 27.9 us (0.88)
  Pallas kernels: 31 us -> 27.1 us
    pallas_call x2, Pallas kernels: 31 us -> 27.1 us  [the longest x1 25.6 us: per_device(): pl.pallas_call(functools.partial(kernel, n_row, n_col), out_shape=tuple((...]
where the time goes in v3:
time: 27.9 us; the launch traced here: 27.7 us
  Pallas kernels  27.1 us (97%)
  between operations  0.64 us (2%)
    pallas_call x1, Pallas kernels, per_device(): pl.pallas_call(functools.partial(kernel, n_row, n_col), out_shape=tuple((...  25.6 us
    pallas_call x1, Pallas kernels, per_device(): pl.pallas_call(copy_out, out_shape=shapes, in_specs=[vmem] * 3, out_specs...  1.43 us

profile of v3, /device:TPU:0, one launch (start us, length us, event | category | flops | bytes accessed | tf_op | source)
XLA Modules:
  0.0 27.7 jit_solution(18000348515053953102)
XLA Ops:
  0.6 25.6 %shard_map.76 = (f32[3,1024]{1,0:T(4,128)S(1)}, f32[3,1024]{1,0:T(4,128)S(1)}, bf16[8,3,3,128,128]{4,3,2,1,0:T(8,128)(2,1)S(1)}) custom-call(bf16[8,3,3,128,128]{4,3,2,1,0:T(8,128)(2,1)} %bitcast.4, s32[2,8]{1,0:T(2,128)} %bitcast.6, f32[8,128]{1,0:T(8,128)} %bitcast.5, f32[3,1024]{1,0:T(4,128)} %field_hbm.1, f32[3,1024]{1,0:T(4,128)} %cot_hbm.1), custom_call_target="tpu_custom_call" | custom-call | tf_op jit(solution)/shard_map/pallas_call | solution.py:308
  26.3 1.4 %shard_map.77 = (f32[3,1024]{1,0:T(4,128)}, f32[3,1024]{1,0:T(4,128)}, bf16[8,3,3,128,128]{4,3,2,1,0:T(8,128)(2,1)}) custom-call(f32[3,1024]{1,0:T(4,128)S(1)} %get-tuple-element.9.refs_0_, f32[3,1024]{1,0:T(4,128)S(1)} %get-tuple-element.10.refs_1_, bf16[8,3,3,128,128]{4,3,2,1,0:T(8,128)(2,1)S(1)} %get-tuple-element.11.refs_2_), custom_call_target="tpu_custom_call" | custom-call | tf_op jit(solution)/shard_map/pallas_call | solution.py:343

commit v4 on v3

--- a/solution.py
+++ b/solution.py
@@ -75,16 +75,24 @@
     ]
     barrier = pltpu.get_barrier_semaphore()
 
+    def far_first(index):
+        return jnp.where(2 * col < n_col, n_col - 1 - index, index)
+
     def greet(index):
-        peer = lax.rem(me + index + 1, group)
-        pl.semaphore_signal(
-            barrier,
-            inc=1,
-            device_id={"row": peer // n_col, "col": lax.rem(peer, n_col)},
-            device_id_type=MESH,
-        )
-
-    repeat(group - 1, greet)
+        other_row = lax.rem(row + n_row // 2 + index, n_row)
+        for k in range(n_col):
+            other_col = far_first(k)
+
+            @pl.when((other_row != row) | (other_col != col))
+            def _():
+                pl.semaphore_signal(
+                    barrier,
+                    inc=1,
+                    device_id={"row": other_row, "col": other_col},
+                    device_id_type=MESH,
+                )
+
+    repeat(n_row, greet)
     for copy in inputs + tile_copies:
         copy.start()
     for copy in inputs:
@@ -195,7 +203,7 @@
             later = summed(target, range(pair_count, 2 * pair_count), second_ids)
             rs_send[step, target] = later.astype(jnp.bfloat16)
             for k in range(n_col):
-                part_copy(step, target, lax.rem(col + k, n_col)).start()
+                part_copy(step, target, far_first(k)).start()
 
         loop(0, n_row - 1 - row, send_later)
 
@@ -219,8 +227,13 @@
             )
         own = (stage[4] + summed(row, range(pair_count), first_ids)).astype(jnp.bfloat16)
         rs_send[step, row] = own
-        for k in range(1, n_col):
-            part_copy(step, row, lax.rem(col + k, n_col)).start()
+        for k in range(n_col):
+            target_col = far_first(k)
+
+            @pl.when(target_col != col)
+            def _():
+                part_copy(step, row, target_col).start()
+
         rs_recv[step, row, col] = own
 
         if step == ITERS - 1:

time: 27.9 us -> 27.5 us (0.986)
  Pallas kernels: 27.1 us -> 26.7 us
    pallas_call x1, Pallas kernels: 25.6 us -> 25.2 us  [per_device(): pl.pallas_call(functools.partial(kernel, n_row, n_col), out_shape=tuple((...]
where the time goes in v4:
time: 27.5 us; the launch traced here: 27.3 us
  Pallas kernels  26.7 us (97%)
  between operations  0.64 us (2%)
    pallas_call x1, Pallas kernels, per_device(): pl.pallas_call(functools.partial(kernel, n_row, n_col), out_shape=tuple((...  25.2 us
    pallas_call x1, Pallas kernels, per_device(): pl.pallas_call(copy_out, out_shape=shapes, in_specs=[vmem] * 3, out_specs...  1.43 us

profile of v4, /device:TPU:0, one launch (start us, length us, event | category | flops | bytes accessed | tf_op | source)
XLA Modules:
  0.0 27.3 jit_solution(4818228265843623083)
XLA Ops:
  0.6 25.2 %shard_map.76 = (f32[3,1024]{1,0:T(4,128)S(1)}, f32[3,1024]{1,0:T(4,128)S(1)}, bf16[8,3,3,128,128]{4,3,2,1,0:T(8,128)(2,1)S(1)}) custom-call(bf16[8,3,3,128,128]{4,3,2,1,0:T(8,128)(2,1)} %bitcast.4, s32[2,8]{1,0:T(2,128)} %bitcast.6, f32[8,128]{1,0:T(8,128)} %bitcast.5, f32[3,1024]{1,0:T(4,128)} %field_hbm.1, f32[3,1024]{1,0:T(4,128)} %cot_hbm.1), custom_call_target="tpu_custom_call" | custom-call | tf_op jit(solution)/shard_map/pallas_call | solution.py:321
  25.9 1.4 %shard_map.77 = (f32[3,1024]{1,0:T(4,128)}, f32[3,1024]{1,0:T(4,128)}, bf16[8,3,3,128,128]{4,3,2,1,0:T(8,128)(2,1)}) custom-call(f32[3,1024]{1,0:T(4,128)S(1)} %get-tuple-element.9.refs_0_, f32[3,1024]{1,0:T(4,128)S(1)} %get-tuple-element.10.refs_1_, bf16[8,3,3,128,128]{4,3,2,1,0:T(8,128)(2,1)S(1)} %get-tuple-element.11.refs_2_), custom_call_target="tpu_custom_call" | custom-call | tf_op jit(solution)/shard_map/pallas_call | solution.py:356

commit v5 on v4

--- a/solution.py
+++ b/solution.py
@@ -36,6 +36,7 @@
     grad,
     tg,
     tiles,
+    turned,
     pairs,
     pol,
     field_in,
@@ -132,10 +133,10 @@
         for b in range(local_blocks):
             fields[step, which_row * local_blocks + b, 0:6, :] = stage[2, 6 * b : 6 * b + 6, :]
 
-    def matrix(p):
+    def matrix(p, held):
         return jnp.concatenate(
             [
-                jnp.concatenate([tiles[p, a, b] for b in range(3)], axis=1)
+                jnp.concatenate([held[p, a, b] for b in range(3)], axis=1)
                 for a in range(3)
             ],
             axis=0,
@@ -192,7 +193,7 @@
                 pair_count + p,
                 lax.dot_general(
                     near,
-                    matrix(p),
+                    matrix(p, tiles),
                     (((1,), (0,)), ((), ())),
                     preferred_element_type=jnp.float32,
                 ),
@@ -206,6 +207,11 @@
                 part_copy(step, target, far_first(k)).start()
 
         loop(0, n_row - 1 - row, send_later)
+        if step == 0:
+            for p in range(pair_count):
+                for a in range(3):
+                    for b in range(3):
+                        turned[p, b, a] = tiles[p, a, b].T
 
         stage[4] = summed(row, range(pair_count, 2 * pair_count), second_ids)
 
@@ -220,8 +226,8 @@
                 p,
                 lax.dot_general(
                     far,
-                    matrix(p),
-                    (((1,), (1,)), ((), ())),
+                    matrix(p, turned),
+                    (((1,), (0,)), ((), ())),
                     preferred_element_type=jnp.float32,
                 ),
             )
@@ -324,6 +330,7 @@
         in_specs=[hbm] * 5,
         out_specs=(vmem,) * 3,
         scratch_shapes=[
+            pltpu.VMEM(tiles.shape, bf16),
             pltpu.VMEM(tiles.shape, bf16),
             pltpu.SMEM((2, pair_count), jnp.int32),
             pltpu.VMEM((local_blocks, block), f32),

time: 27.5 us -> 27.2 us (0.989)
  Pallas kernels: 26.7 us -> 26.4 us
where the time goes in v5:
time: 27.2 us; the launch traced here: 27.1 us
  Pallas kernels  26.4 us (97%)
  between operations  0.64 us (2%)
    pallas_call x1, Pallas kernels, per_device(): pl.pallas_call(functools.partial(kernel, n_row, n_col), out_shape=tuple((...  25 us
    pallas_call x1, Pallas kernels, per_device(): pl.pallas_call(copy_out, out_shape=shapes, in_specs=[vmem] * 3, out_specs...  1.43 us

profile of v5, /device:TPU:0, one launch (start us, length us, event | category | flops | bytes accessed | tf_op | source)
XLA Modules:
  0.0 27.1 jit_solution(5627309104986362190)
XLA Ops:
  0.6 25.0 %shard_map.76 = (f32[3,1024]{1,0:T(4,128)S(1)}, f32[3,1024]{1,0:T(4,128)S(1)}, bf16[8,3,3,128,128]{4,3,2,1,0:T(8,128)(2,1)S(1)}) custom-call(bf16[8,3,3,128,128]{4,3,2,1,0:T(8,128)(2,1)} %bitcast.4, s32[2,8]{1,0:T(2,128)} %bitcast.6, f32[8,128]{1,0:T(8,128)} %bitcast.5, f32[3,1024]{1,0:T(4,128)} %field_hbm.1, f32[3,1024]{1,0:T(4,128)} %cot_hbm.1), custom_call_target="tpu_custom_call" | custom-call | tf_op jit(solution)/shard_map/pallas_call | solution.py:327
  25.6 1.4 %shard_map.77 = (f32[3,1024]{1,0:T(4,128)}, f32[3,1024]{1,0:T(4,128)}, bf16[8,3,3,128,128]{4,3,2,1,0:T(8,128)(2,1)}) custom-call(f32[3,1024]{1,0:T(4,128)S(1)} %get-tuple-element.9.refs_0_, f32[3,1024]{1,0:T(4,128)S(1)} %get-tuple-element.10.refs_1_, bf16[8,3,3,128,128]{4,3,2,1,0:T(8,128)(2,1)S(1)} %get-tuple-element.11.refs_2_), custom_call_target="tpu_custom_call" | custom-call | tf_op jit(solution)/shard_map/pallas_call | solution.py:363
